TPU v7x, 128 devices: a whole 4x4x4 slice. The times are simulated.
128 devices in a mesh: row: 8 (over x, y_lo), col: 16 (over z, y_hi, core).
Axes of the slice: x: 4, y: 4 (y_hi: 2, y_lo: 2; y = y_hi * 2 + y_lo), z: 4, core: 2. Of those that a mesh axis runs over, the one named last changes fastest.
Arguments:
- halves: float32 [2, 4096, 16384], P(None, 'row', 'col'), may hold values from -6 to 6
- diag_rest: float32 [8192, 1024], P(('col', 'row')), may hold values from -6 to 6
- panel_vectors: float32 [16384, 256], P('col'), may hold values from -1 to 1
- tri_factor: float32 [256, 256], replicated, may hold values from -1 to 2, as said below
Outputs:
- updated_halves: float32 [2, 4096, 16384], P(None, 'row', 'col')
- updated_rest: float32 [8192, 1024], P(('col', 'row'))
- w_panel: float32 [16384, 256], P('col')
Inputs may be any that keep to these rules, and one draw needn't show every extreme that they name: `tri_factor`: upper triangular, diagonal between 1 and 2.
All inputs are finite; a program needn't handle non-finite values.
Results may differ from a plain program's by a relative error of at most 0.0003.
Values sent between devices are 32-bit elements; how exact they have to be, the bound alone decides.
A program may use at most 64 MiB of HBM per device.

v0:
```python
import jax
import jax.numpy as jnp
from jax import lax
from jax.sharding import PartitionSpec as P

precise = lax.Precision.HIGHEST


def broadcast(value, axis, source):
    kept = jnp.where(lax.axis_index(axis) == source, value, 0).astype(value.dtype)
    return lax.psum(kept, axis)


def matmul(left, right):
    return jnp.dot(left, right, precision=precise, preferred_element_type=jnp.float32)


def left_contract(left, right):
    return lax.dot_general(
        left, right, (((0,), (0,)), ((), ())), precision=precise, preferred_element_type=jnp.float32
    )


def right_contract(left, right):
    return lax.dot_general(
        left, right, (((1,), (1,)), ((), ())), precision=precise, preferred_element_type=jnp.float32
    )


def shards(halves, diag_rest, panel_vectors, tri_factor):
    row_count = lax.axis_size("row")
    row_index = lax.axis_index("row")
    col_index = lax.axis_index("col")
    half_size = halves.shape[1]
    tile_size = halves.shape[2]
    panel_width = panel_vectors.shape[1]
    rest_rows = diag_rest.shape[0]
    rest_start = half_size + row_index * rest_rows
    zero_block = jnp.zeros((tile_size, panel_width), jnp.float32)
    row_vecs = []
    for position in range(2):
        row_vecs.append(broadcast(panel_vectors, "col", row_index + row_count * position))
    layout = []
    row_parts = []
    col_part = zero_block
    for position in range(2):
        block_row = row_index + row_count * position
        is_lower = block_row >= col_index
        weight = jnp.where(block_row == col_index, 0.5, 1.0).astype(jnp.float32)
        offset = jnp.where(is_lower, 0, half_size).astype(jnp.int32)
        low_vec = jnp.where(is_lower, panel_vectors, row_vecs[position])
        high_vec = jnp.where(is_lower, row_vecs[position], panel_vectors)
        high_half = lax.dynamic_slice_in_dim(high_vec, offset, half_size, 0)
        first = matmul(halves[position], low_vec) * weight
        second = left_contract(halves[position], high_half) * weight
        padded = lax.dynamic_update_slice_in_dim(zero_block, first, offset, 0)
        row_parts.append(jnp.where(is_lower, padded, second))
        col_part = col_part + jnp.where(is_lower, second, padded)
        layout.append((block_row, is_lower, offset, low_vec, high_half))
    own_rest_vec = lax.dynamic_slice_in_dim(panel_vectors, rest_start, rest_rows, 0)
    rest_first = lax.dynamic_update_slice_in_dim(
        zero_block, matmul(diag_rest, panel_vectors), rest_start, 0
    )
    col_part = col_part + 0.5 * (rest_first + left_contract(diag_rest, own_rest_vec))
    row_totals = lax.psum(jnp.stack(row_parts), "col")
    extra = zero_block
    for position in range(2):
        block_row = row_index + row_count * position
        extra = extra + jnp.where(block_row == col_index, row_totals[position], 0.0)
    col_terms = col_part + extra
    av_block = lax.psum(col_terms, "row")
    inner = lax.psum(left_contract(panel_vectors, av_block), "col")
    middle = matmul(left_contract(tri_factor, inner), tri_factor)
    w_own = matmul(av_block, tri_factor) - 0.5 * matmul(panel_vectors, middle)
    row_ws = []
    for position in range(2):
        row_ws.append(broadcast(w_own, "col", row_index + row_count * position))
    updated = []
    for position in range(2):
        block_row, is_lower, offset, low_vec, high_half = layout[position]
        low_w = jnp.where(is_lower, w_own, row_ws[position])
        high_w = jnp.where(is_lower, row_ws[position], w_own)
        high_whalf = lax.dynamic_slice_in_dim(high_w, offset, half_size, 0)
        left = jnp.concatenate([high_half, high_whalf], 1)
        right = jnp.concatenate([low_w, low_vec], 1)
        updated.append(halves[position] - right_contract(left, right))
    own_rest_w = lax.dynamic_slice_in_dim(w_own, rest_start, rest_rows, 0)
    left_rest = jnp.concatenate([own_rest_vec, own_rest_w], 1)
    right_rest = jnp.concatenate([w_own, panel_vectors], 1)
    new_rest = diag_rest - right_contract(left_rest, right_rest)
    return (jnp.stack(updated), new_rest, w_own)


def solution(mesh):
    return jax.shard_map(
        shards,
        mesh=mesh,
        in_specs=(P(None, "row", "col"), P(("col", "row"), None), P("col", None), P()),
        out_specs=(P(None, "row", "col"), P(("col", "row"), None), P("col", None)),
        check_vma=False,
    )
```

profile of v0, /device:TPU:0, one launch (start us, length us, event | category | flops | bytes accessed | tf_op | source)
XLA Modules:
  0.0 716.4 jit_solution(4993959610792432966)
XLA Ops:
  7.2 1.6 copy.7
  8.8 1.6 broadcast_select_fusion.3
  10.6 149.7 %all-reduce.16.cloned.1.call-done = (f32[1024,256]{0,1:T(8,128)}, f32[1024,256]{0,1:T(8,128)}) async-done(((f32[1024,256]{0,1:T(8,128)}, f32[1024,256]{0,1:T(8,128)}), (f32[1024,256]{0,1:T(8,128)}, f32[1024,256]{0,1:T(8,128)})) %all-reduce.16.cloned.1.call-update) | async-done | bytes 2097168 | tf_op jit(solution)/shard_map/psum | solution.py:11
  160.6 0.9 copy-done.18
  161.5 2.3 dynamic-slice_select_fusion.3
  163.9 1.9 fusion.35
  165.8 1.9 fusion.41
  167.9 1.9 fusion.50
  170.0 1.9 fusion.59
  171.9 0.4 select_bitcast_fusion
  172.3 1.5 pad_maximum_fusion.1
  174.2 1.9 fusion.80
  176.1 1.0 copy-done.11
  177.1 3.4 convolution_add_fusion
  180.5 1.8 add.59
  182.2 138.8 %all-reduce.8.cloned.1.call-done = f32[2,1024,256]{1,2,0:T(8,128)} async-done(((f32[2,1024,256]{1,2,0:T(8,128)}), f32[2,1024,256]{1,2,0:T(8,128)}) %all-reduce.8.cloned.1.call-update) | async-done | bytes 2097168 | tf_op jit(solution)/shard_map/psum | solution.py:65
  321.0 4.3 fusion.67
  325.4 77.6 %all-reduce.10.cloned.1.call-done = f32[1024,256]{0,1:T(8,128)} async-done(((f32[1024,256]{0,1:T(8,128)}), f32[1024,256]{0,1:T(8,128)}) %all-reduce.10.cloned.1.call-update) | async-done | bytes 1048592 | tf_op jit(solution)/shard_map/psum | solution.py:71
  403.0 3.0 convolution_bitcast_fusion
  406.1 2.1 fusion.81
  408.2 134.5 %all-reduce.12.cloned.1.call-done = f32[256,256]{0,1:T(8,128)} async-done(((f32[256,256]{0,1:T(8,128)}), f32[256,256]{0,1:T(8,128)}) %all-reduce.12.cloned.1.call-update) | async-done | bytes 262160 | tf_op jit(solution)/shard_map/psum | solution.py:72
  542.7 1.4 fusion.82
  544.2 0.6 fusion.83
  544.8 3.3 broadcast_select_fusion.1
  548.1 1.3 copy.17
  549.6 2.1 fusion.62
  551.7 144.4 %all-reduce.14.cloned.1.call-done = (f32[1024,256]{0,1:T(8,128)}, f32[1024,256]{0,1:T(8,128)}) async-done(((f32[1024,256]{0,1:T(8,128)}, f32[1024,256]{0,1:T(8,128)}), (f32[1024,256]{0,1:T(8,128)}, f32[1024,256]{0,1:T(8,128)})) %all-reduce.14.cloned.1.call-update) | async-done | bytes 2097168 | tf_op jit(solution)/shard_map/psum | solution.py:11
  696.1 1.6 dynamic-slice_select_fusion.1
  698.2 1.9 copy-done.2
  700.4 3.5 fusion.21
  704.0 3.6 fusion.16
  707.6 2.3 pad_maximum_fusion
  (57 shorter events, 2.1 us)
Async XLA Ops:
  7.2 399.0 %copy-start = (f32[256,256]{1,0:T(8,128)S(1)}, f32[256,256]{1,0:T(8,128)}, u32[]{:S(2)}) copy-start(f32[256,256]{1,0:T(8,128)} %param.7) | copy-start | bytes 786436
  7.2 153.1 %all-reduce.16.cloned.1.call-start = ((), (), s32[]{:S(2)}) async-start(), calls=%async_computation.4 | async-start | bytes 4194304 | tf_op jit(solution)/shard_map/psum | solution.py:11
  10.5 310.5 %all-reduce.8.cloned.1.call-start = ((), (), s32[]{:S(2)}) async-start(), calls=%async_computation | async-start | bytes 4194304 | tf_op jit(solution)/shard_map/psum | solution.py:65
  160.3 1.2 copy-start.18
  160.3 3.6 copy-start.1
  161.5 6.4 copy-start.7
  161.5 8.4 %copy-start.5 = (f32[1024,256]{0,1:T(8,128)}, f32[1024,256]{0,1:T(8,128)S(1)}, u32[]{:S(2)}) copy-start(f32[1024,256]{0,1:T(8,128)S(1)} %get-tuple-element.19) | copy-start | bytes 3145732
  163.8 3.9 copy-start.12
  163.8 3.9 copy-start.14
  165.8 6.1 copy-start.9
  167.7 4.2 copy-start.10
  169.8 2.1 copy-start.4
  173.8 3.3 copy-start.3
  173.8 229.2 %all-reduce.10.cloned.1.call-start = ((), (), s32[]{:S(2)}) async-start(), calls=%async_computation.1 | async-start | bytes 2097152 | tf_op jit(solution)/shard_map/psum | solution.py:71
  176.1 1.0 copy-start.11
  325.3 217.4 %all-reduce.12.cloned.1.call-start = ((), (), s32[]{:S(2)}) async-start(), calls=%async_computation.2 | async-start | bytes 524288 | tf_op jit(solution)/shard_map/psum | solution.py:72
  403.0 3.1 copy-start.16
  406.1 290.0 %all-reduce.14.cloned.1.call-start = ((), (), s32[]{:S(2)}) async-start(), calls=%async_computation.3 | async-start | bytes 4194304 | tf_op jit(solution)/shard_map/psum | solution.py:11
  542.7 2.0 copy-start.17
  548.1 1.4 copy-start.21
  696.1 1.6 copy-start.19
  696.1 1.9 copy-start.20
  696.1 2.1 copy-start.15
  697.9 2.2 copy-start.2
  697.9 2.5 copy-start.8
  700.4 3.5 copy-start.6
  700.4 3.6 copy-start.13
Sparse Core Ops, SparseCore 0:
  11.1 149.0 all-reduce.15
  173.9 147.0 all-reduce.7
  325.5 77.5 all-reduce.9
  406.2 136.5 all-reduce.11
  548.3 147.7 all-reduce.13
where the time goes:
time: 717 us; the launch traced here: 716 us
  waiting for transfers between devices  645 us (90%)
  matrix products  32.7 us (5%)
  other arithmetic  14.6 us (2%)
  between operations  14.1 us (2%)
  local copies, waits for them, and re-layouts  9.56 us (1%)
    psum x2, waiting for transfers between devices, broadcast(): return lax.psum(kept, axis)  294 us
    psum x1, waiting for transfers between devices, shards(): row_totals = lax.psum(jnp.stack(row_parts), 'col')  139 us
    psum x1, waiting for transfers between devices, shards(): inner = lax.psum(left_contract(panel_vectors, av_block), 'col')  135 us
    psum x1, waiting for transfers between devices, shards(): av_block = lax.psum(col_terms, 'row')  77.6 us
  transfers between devices with their start and end apart: 5, of which 5 were waited for; matrix products, arithmetic and copies ran while one was open for 2% of the time, Pallas kernels for 0%

commit v1 on v0

--- a/solution.py
+++ b/solution.py
@@ -62,7 +62,7 @@
         zero_block, matmul(diag_rest, panel_vectors), rest_start, 0
     )
     col_part = col_part + 0.5 * (rest_first + left_contract(diag_rest, own_rest_vec))
-    row_totals = lax.psum(jnp.stack(row_parts), "col")
+    row_totals = jnp.sum(lax.all_gather(jnp.stack(row_parts), "col"), axis=0)
     extra = zero_block
     for position in range(2):
         block_row = row_index + row_count * position

time: 717 us -> 778 us (1.085)
  waiting for transfers between devices: 645 us -> 682 us
  other arithmetic: 14.6 us -> 27.6 us
  local copies, waits for them, and re-layouts: 9.56 us -> 21.1 us
    all_gather x0 -> x1, waiting for transfers between devices: none -> 179 us  [shards(): row_totals = jnp.sum(lax.all_gather(jnp.stack(row_parts), 'col'), axis=0)]
    psum x1 -> x0, waiting for transfers between devices: 139 us -> none  [shards(): row_totals = lax.psum(jnp.stack(row_parts), 'col')]
    reduce_sum x0 -> x1, other arithmetic: none -> 13.4 us  [shards(): row_totals = jnp.sum(lax.all_gather(jnp.stack(row_parts), 'col'), axis=0)]
where the time goes in v1:
time: 778 us
  waiting for transfers between devices  682 us (88%)
  matrix products  32.7 us (4%)
  other arithmetic  27.6 us (4%)
  local copies, waits for them, and re-layouts  21.1 us (3%)
  between operations  14.1 us (2%)
    psum x2, waiting for transfers between devices, broadcast(): return lax.psum(kept, axis)  294 us
    all_gather x1, waiting for transfers between devices, shards(): row_totals = jnp.sum(lax.all_gather(jnp.stack(row_parts), 'col'), axis=0)  179 us
    psum x1, waiting for transfers between devices, shards(): inner = lax.psum(left_contract(panel_vectors, av_block), 'col')  135 us
    psum x1, waiting for transfers between devices, shards(): av_block = lax.psum(col_terms, 'row')  74.7 us
  transfers between devices with their start and end apart: 5, of which 5 were waited for; matrix products, arithmetic and copies ran while one was open for 2% of the time, Pallas kernels for 0%

profile of v1, /device:TPU:0, one launch (start us, length us, event | category | flops | bytes accessed | tf_op | source)
XLA Modules:
  0.0 777.7 jit_solution(10325205442690874482)
XLA Ops:
  7.2 1.6 copy.30
  8.8 1.6 broadcast_select_fusion.3
  10.6 149.7 %all-reduce.13.cloned.1.call-done = (f32[1024,256]{0,1:T(8,128)}, f32[1024,256]{0,1:T(8,128)}) async-done(((f32[1024,256]{0,1:T(8,128)}, f32[1024,256]{0,1:T(8,128)}), (f32[1024,256]{0,1:T(8,128)}, f32[1024,256]{0,1:T(8,128)})) %all-reduce.13.cloned.1.call-update) | async-done | bytes 2097168 | tf_op jit(solution)/shard_map/psum | solution.py:11
  161.5 2.3 dynamic-slice_select_fusion.3
  163.9 1.9 fusion.35
  165.8 1.9 fusion.41
  167.9 1.9 fusion.50
  169.9 1.9 fusion.59
  172.9 1.5 pad_maximum_fusion.1
  174.4 2.9 copy.38
  177.6 1.9 fusion.78
  180.6 3.4 convolution_add_fusion
  184.0 1.8 add.57
  185.8 178.5 %all-gather.3.cloned.1.call-done = f32[32,1024,256]{2,1,0:T(8,128)} async-done(((f32[2,1024,256]{2,1,0:T(8,128)}), f32[32,1024,256]{2,1,0:T(8,128)}) %all-gather.3.cloned.1.call-update) | async-done | bytes 33554448 | tf_op jit(solution)/shard_map/all_gather | solution.py:65
  364.3 13.4 %reduce_sum.9 = f32[2,1024,256]{2,1,0:T(8,128)} reduce(f32[16,2,1024,256]{3,2,1,0:T(8,128)} %bitcast.86, f32[]{:T(128)} %constant.8.clone.1), dimensions={0}, to_apply=%region_2.3 | reduce | flops 7864320 | bytes 35651588 | tf_op jit(solution)/shard_map/reduce_sum | solution.py:65
  377.7 3.0 fusion.77
  380.7 2.5 copy.46
  383.2 2.5 copy.47
  385.7 4.0 bitcast_add_fusion
  389.8 74.7 %all-reduce.7.cloned.1.call-done = f32[1024,256]{0,1:T(8,128)} async-done(((f32[1024,256]{0,1:T(8,128)}), f32[1024,256]{0,1:T(8,128)}) %all-reduce.7.cloned.1.call-update) | async-done | bytes 1048592 | tf_op jit(solution)/shard_map/psum | solution.py:71
  464.5 3.0 convolution_bitcast_fusion
  467.6 2.1 fusion.79
  469.7 134.5 %all-reduce.9.cloned.1.call-done = f32[256,256]{0,1:T(8,128)} async-done(((f32[256,256]{0,1:T(8,128)}), f32[256,256]{0,1:T(8,128)}) %all-reduce.9.cloned.1.call-update) | async-done | bytes 262160 | tf_op jit(solution)/shard_map/psum | solution.py:72
  604.2 1.4 fusion.80
  606.3 3.3 broadcast_select_fusion.1
  611.0 2.1 fusion.62
  613.2 144.1 %all-reduce.11.cloned.1.call-done = (f32[1024,256]{0,1:T(8,128)}, f32[1024,256]{0,1:T(8,128)}) async-done(((f32[1024,256]{0,1:T(8,128)}, f32[1024,256]{0,1:T(8,128)}), (f32[1024,256]{0,1:T(8,128)}, f32[1024,256]{0,1:T(8,128)})) %all-reduce.11.cloned.1.call-update) | async-done | bytes 2097168 | tf_op jit(solution)/shard_map/psum | solution.py:11
  757.3 1.6 dynamic-slice_select_fusion.1
  759.4 1.9 copy-done.2
  761.6 3.6 fusion.21
  765.2 3.6 fusion.16
  768.8 2.3 pad_maximum_fusion
  (62 shorter events, 6.9 us)
Async XLA Ops:
  7.2 460.5 %copy-start = (f32[256,256]{1,0:T(8,128)S(1)}, f32[256,256]{1,0:T(8,128)}, u32[]{:S(2)}) copy-start(f32[256,256]{1,0:T(8,128)} %param.7) | copy-start | bytes 786436
  7.2 153.1 %all-reduce.13.cloned.1.call-start = ((), (), s32[]{:S(2)}) async-start(), calls=%async_computation.4 | async-start | bytes 4194304 | tf_op jit(solution)/shard_map/psum | solution.py:11
  10.5 353.8 %all-gather.3.cloned.1.call-start = ((), (), s32[]{:S(2)}) async-start(), calls=%async_computation.2 | async-start | bytes 35651584 | tf_op jit(solution)/shard_map/all_gather | solution.py:65
  160.3 1.2 copy-start.18
  160.3 3.6 copy-start.1
  161.5 6.4 copy-start.7
  161.5 8.4 %copy-start.5 = (f32[1024,256]{0,1:T(8,128)}, f32[1024,256]{0,1:T(8,128)S(1)}, u32[]{:S(2)}) copy-start(f32[1024,256]{0,1:T(8,128)S(1)} %get-tuple-element.27) | copy-start | bytes 3145732
  163.8 3.9 copy-start.12
  163.8 3.9 copy-start.14
  165.8 6.1 copy-start.9
  167.7 4.2 copy-start.10
  171.9 1.0 copy-start.4
  177.2 3.3 copy-start.3
  177.3 287.2 %all-reduce.7.cloned.1.call-start = ((), (), s32[]{:S(2)}) async-start(), calls=%async_computation | async-start | bytes 2097152 | tf_op jit(solution)/shard_map/psum | solution.py:71
  179.5 1.0 copy-start.11
  389.8 214.5 %all-reduce.9.cloned.1.call-start = ((), (), s32[]{:S(2)}) async-start(), calls=%async_computation.1 | async-start | bytes 524288 | tf_op jit(solution)/shard_map/psum | solution.py:72
  464.5 3.1 copy-start.16
  467.6 289.7 %all-reduce.11.cloned.1.call-start = ((), (), s32[]{:S(2)}) async-start(), calls=%async_computation.3 | async-start | bytes 4194304 | tf_op jit(solution)/shard_map/psum | solution.py:11
  604.2 2.0 copy-start.17
  609.6 1.4 copy-start.21
  757.3 1.6 copy-start.19
  757.3 1.9 copy-start.20
  757.3 2.1 copy-start.15
  759.1 2.2 copy-start.2
  759.1 2.5 copy-start.8
  761.6 3.6 copy-start.6
  761.6 3.6 copy-start.13
Sparse Core Ops, SparseCore 0:
  11.1 149.0 all-reduce.12
  177.4 186.8 all-gather.2
  389.9 74.5 all-reduce.6
  467.7 136.5 all-reduce.8
  609.7 147.4 all-reduce.10
